TPU v7x, 32 devices: a whole 2x2x4 slice. The times are simulated.
32 devices in a mesh: row: 4 (over y, core), col: 8 (over z, x).
Axes of the slice: x: 2, y: 2, z: 4, core: 2. Of those that a mesh axis runs over, the one named last changes fastest.
Arguments:
- features: bfloat16 [16, 524288], P(None, ('row', 'col')), may hold values from -6 to 6
- point_weights: bfloat16 [8, 524288], P(None, ('row', 'col')), may hold values from 0.049804688 to 1
- point_corner: int32 [524288], P(('row', 'col')), may hold values from 0 to 342
- block_owner: int32 [4096, 1], P(('row', 'col')), may hold values from 0 to 31; in each aligned block of 128 rows (0 to 127, 128 to 255, ...) at most 8 rows name the same one
- block_cell: int32 [4096], P(('row', 'col')), may hold values from 0 to 1023
- spec_weight: bfloat16 [64, 64, 16, 16, 128], P('col', 'row'), may hold values from -12 to 12
- skip_weight: bfloat16 [16, 16], replicated, may hold values from -1.5 to 1.5
- mlp_in: bfloat16 [64, 16], replicated, may hold values from -1.5 to 1.5
- mlp_bias: float32 [64], replicated, may hold values from -4 to 4
- mlp_out: bfloat16 [16, 64], replicated, may hold values from -0.75 to 0.75
Outputs:
- point_values: bfloat16 [16, 524288], P(None, ('row', 'col'))
Inputs may be any that keep to these rules, and one draw needn't show every extreme that they name: `block_owner`: in each aligned block of 128 rows (the point blocks of one device) no device number appears more than 8 times; devices are numbered r * 8 + s over row r and column s.
All inputs are finite; a program needn't handle non-finite values.
Results may differ from a plain program's by a relative error of at most 0.013.
Values may be sent and summed in bfloat16 or wider, within the bound.
A program may use at most 320 MiB of HBM per device.

v0:
```python
import math

import jax
import jax.numpy as jnp
from jax import lax
from jax.sharding import PartitionSpec as P

GRID = 256
BE = 8
PB_PTS = 128


def frequencies(count, length):
    index = jnp.arange(count, dtype=jnp.int32)
    return jnp.where(index < count // 2, index, length - count + index)


def angles(length, freq):
    places = jnp.arange(length, dtype=jnp.int32)
    turns = places[:, None] * freq[None, :] % length
    return 2.0 * math.pi / length * turns.astype(jnp.float32)


def forward_tables(length, count):
    factor = 1.0 / math.sqrt(length)
    theta = angles(length, jnp.arange(count, dtype=jnp.int32))
    real_basis_table = jnp.stack([jnp.cos(theta) * factor, -jnp.sin(theta) * factor], -1).reshape(
        length, 2 * count
    )
    theta = angles(length, frequencies(count, length))
    cosine = jnp.cos(theta) * factor
    sine = jnp.sin(theta) * factor
    from_real = jnp.stack([cosine, -sine], -1)
    from_imag = jnp.stack([sine, cosine], -1)
    paired = jnp.stack([from_real, from_imag], 0)
    planar = jnp.swapaxes(paired, 2, 3)
    return (
        real_basis_table.astype(jnp.bfloat16),
        paired.reshape(2, length, 2 * count).astype(jnp.bfloat16),
        planar.reshape(2, length, 2 * count).astype(jnp.bfloat16),
    )


def inverse_tables(length, count):
    factor = 1.0 / math.sqrt(length)
    theta = angles(length, frequencies(count, length)).T
    cosine = jnp.cos(theta) * factor
    sine = jnp.sin(theta) * factor
    from_real = jnp.stack([cosine, sine], 1)
    from_imag = jnp.stack([-sine, cosine], 1)
    paired = jnp.stack([from_real, from_imag], 1)
    planar = jnp.swapaxes(paired, 0, 1)
    theta = angles(length, jnp.arange(count, dtype=jnp.int32)).T
    double = jnp.where(jnp.arange(count) == 0, 1.0, 2.0).astype(jnp.float32)[:, None]
    real_out = jnp.stack([double * jnp.cos(theta) * factor, -double * jnp.sin(theta) * factor], 1)
    return (
        real_out.reshape(2 * count, length).astype(jnp.bfloat16),
        paired.reshape(2 * count, 2, length).astype(jnp.bfloat16),
        planar.reshape(2 * count, 2, length).astype(jnp.bfloat16),
    )


def corner_cell_indices(point_corner, edge_len):
    interior = edge_len - 1
    anchor = point_corner // (interior * interior) * edge_len * edge_len
    anchor = anchor + point_corner // interior % interior * edge_len + point_corner % interior
    corners = jnp.arange(8, dtype=jnp.int32)
    offsets = corners // 4 * edge_len * edge_len + corners // 2 % 2 * edge_len + corners % 2
    return anchor[None, :] + offsets[:, None]


def weighted_onehot(cell_index, weights, block_cells):
    lanes = jnp.arange(block_cells, dtype=jnp.int32)
    return jnp.where(
        cell_index[..., None] == lanes, weights[..., None], jnp.zeros((), jnp.bfloat16)
    )


def spread_point_group(args):
    feature_rows, cell_index, weights = args
    basis_table = weighted_onehot(cell_index, weights, BE**3)
    return jnp.einsum(
        "eqf,esfx->eqx", feature_rows, basis_table, preferred_element_type=jnp.float32
    ).astype(jnp.bfloat16)


def gather_group(args):
    value_entries, cell_index, weights = args
    basis_table = weighted_onehot(cell_index, weights, value_entries.shape[-1])
    return jnp.einsum(
        "zsx,zhvx->zsv", value_entries, basis_table, preferred_element_type=jnp.float32
    ).astype(jnp.bfloat16)


def grouped(array, group):
    return array.reshape((array.shape[0] // group, group) + array.shape[1:])


def mix_modes(spectrum, weight):
    half = weight.shape[-1] // 2
    value_entries = spectrum.astype(jnp.float32)
    coeffs = weight.astype(jnp.float32)
    swapped = jnp.concatenate([value_entries[..., half:], value_entries[..., :half]], -1)
    real_part = jnp.concatenate([coeffs[..., :half], coeffs[..., :half]], -1)
    imag_part = jnp.concatenate([-coeffs[..., half:], coeffs[..., half:]], -1)
    total = value_entries[..., :, None, :] * real_part + swapped[..., :, None, :] * imag_part
    return jnp.sum(total, axis=-3).astype(jnp.bfloat16)


def body(
    features,
    point_weights,
    point_corner,
    block_owner,
    block_cell,
    spec_weight,
    skip_weight,
    mlp_in,
    mlp_bias,
    mlp_out,
):
    row_count = lax.axis_size("row")
    col_count = lax.axis_size("col")
    devices = row_count * col_count
    channels = features.shape[0]
    block_count = block_cell.shape[0]
    block_points = PB_PTS
    edge_len = BE
    block_cells = edge_len**3
    grid_len = GRID
    mode_count = spec_weight.shape[-1] // 2
    capacity = max(2, (2 * block_count + devices - 1) // devices)
    slot_total = devices * capacity
    x_local = grid_len // row_count
    y_local = grid_len // col_count
    x_blocks = x_local // edge_len
    y_blocks = y_local // edge_len
    z_blocks = grid_len // edge_len
    local_blocks = x_blocks * y_blocks * z_blocks
    group = math.gcd(block_count, 8)
    cell_index = corner_cell_indices(point_corner, edge_len)
    grouped_cell_lists = cell_index.reshape(8, block_count // group, group, block_points).transpose(
        1, 2, 0, 3
    )
    weight_groups = point_weights.reshape(8, block_count // group, group, block_points).transpose(
        1, 2, 0, 3
    )
    owner = block_owner[:, 0]
    block_ids = jnp.arange(block_count, dtype=jnp.int32)
    earlier = block_ids[None, :] < block_ids[:, None]
    rank = jnp.sum((owner[None, :] == owner[:, None]) & earlier, axis=1)
    slot = owner * capacity + rank
    slot_ids = jnp.arange(slot_total, dtype=jnp.int32)
    match = slot[None, :] == slot_ids[:, None]
    filled = jnp.any(match, axis=1)
    block_of_slot = jnp.sum(jnp.where(match, block_ids[None, :], 0), axis=1)
    send_ids = jnp.where(filled, block_cell[block_of_slot] + 1, 0).reshape(devices, capacity)
    feat_groups = features.reshape(channels, block_count // group, group, block_points).transpose(
        1, 2, 0, 3
    )
    partial_value = lax.map(spread_point_group, (feat_groups, grouped_cell_lists, weight_groups))
    partial_value = partial_value.reshape(block_count, channels, block_cells)
    send_vals = jnp.where(
        filled[:, None, None], partial_value[block_of_slot], jnp.zeros((), jnp.bfloat16)
    )
    send_vals = send_vals.reshape(devices, capacity, channels, block_cells)
    got_vals, got_ids = (
        lax.all_to_all(send_vals, ("row", "col"), split_axis=0, concat_axis=0, tiled=True),
        lax.all_to_all(send_ids, ("row", "col"), split_axis=0, concat_axis=0, tiled=True),
    )
    got_vals = got_vals.reshape(slot_total, channels, block_cells)
    got_ids = got_ids.reshape(slot_total)
    local_ids = jnp.arange(local_blocks, dtype=jnp.int32)
    landing = (got_ids[None, :] - 1 == local_ids[:, None]).astype(jnp.bfloat16)
    blocks = jnp.einsum(
        "ls,scu->lcu", landing, got_vals, preferred_element_type=jnp.float32
    ).astype(jnp.bfloat16)
    field = blocks.reshape(x_blocks, y_blocks, z_blocks, channels, edge_len, edge_len, edge_len)
    field = field.transpose(3, 0, 4, 1, 5, 2, 6).reshape(channels, x_local, y_local, grid_len)
    table_z, table_y, table_x = forward_tables(grid_len, mode_count)
    inv_z, inv_y, inv_x = inverse_tables(grid_len, mode_count)
    zspec = jnp.einsum("cxyz,zq->cxyq", field, table_z, preferred_element_type=jnp.float32).astype(
        jnp.bfloat16
    )
    zspec = zspec.transpose(3, 2, 0, 1).reshape(2 * mode_count, y_local, channels * x_local)
    zspec = lax.all_to_all(zspec, "col", split_axis=0, concat_axis=1, tiled=True)
    kz_local = zspec.shape[0] // 2
    yspec = jnp.einsum(
        "kpyr,pyq->kqr",
        zspec.reshape(kz_local, 2, grid_len, channels * x_local),
        table_y,
        preferred_element_type=jnp.float32,
    ).astype(jnp.bfloat16)
    yspec = yspec.reshape(kz_local, 2 * mode_count, channels, x_local)
    yspec = lax.all_to_all(yspec, "row", split_axis=1, concat_axis=3, tiled=True)
    ky_local = yspec.shape[1] // 2
    spectrum = jnp.einsum(
        "kjpcx,pxq->kjcq",
        yspec.reshape(kz_local, ky_local, 2, channels, grid_len),
        table_x,
        preferred_element_type=jnp.float32,
    ).astype(jnp.bfloat16)
    mixed = mix_modes(spectrum, spec_weight)
    xinv = jnp.einsum("kjoq,qpx->kjpox", mixed, inv_x, preferred_element_type=jnp.float32).astype(
        jnp.bfloat16
    )
    xinv = xinv.reshape(kz_local, 2 * ky_local, channels, grid_len)
    xinv = lax.all_to_all(xinv, "row", split_axis=3, concat_axis=1, tiled=True)
    yinv = jnp.einsum(
        "kqr,qpy->kpyr",
        xinv.reshape(kz_local, 2 * mode_count, channels * x_local),
        inv_y,
        preferred_element_type=jnp.float32,
    ).astype(jnp.bfloat16)
    yinv = yinv.reshape(2 * kz_local, grid_len, channels * x_local)
    yinv = lax.all_to_all(yinv, "col", split_axis=1, concat_axis=0, tiled=True)
    yinv = yinv.reshape(2 * mode_count, y_local, channels, x_local).transpose(2, 3, 1, 0)
    spectral = jnp.einsum("cxyq,qz->cxyz", yinv, inv_z, preferred_element_type=jnp.float32)
    pre = spectral + jnp.einsum(
        "oi,ixyz->oxyz", skip_weight, field, preferred_element_type=jnp.float32
    )
    pre = pre.astype(jnp.bfloat16)
    hidden = (
        jnp.einsum("hi,ixyz->hxyz", mlp_in, pre, preferred_element_type=jnp.float32)
        + mlp_bias[:, None, None, None]
    )
    hidden = jax.nn.gelu(hidden).astype(jnp.bfloat16)
    layer_field = jnp.einsum(
        "oh,hxyz->oxyz", mlp_out, hidden, preferred_element_type=jnp.float32
    ).astype(jnp.bfloat16)
    layer_grid = layer_field.reshape(
        channels, x_blocks, edge_len, y_blocks, edge_len, z_blocks, edge_len
    )
    layer_grid = layer_grid.transpose(1, 3, 5, 0, 2, 4, 6).reshape(
        local_blocks, channels, block_cells
    )
    present = got_ids > 0
    owned_vals = jnp.where(
        present[:, None, None], layer_grid[jnp.maximum(got_ids - 1, 0)], jnp.zeros((), jnp.bfloat16)
    )
    owned_vals = owned_vals.reshape(devices, capacity, channels, block_cells)
    returned = lax.all_to_all(owned_vals, ("row", "col"), split_axis=0, concat_axis=0, tiled=True)
    mine = returned.reshape(slot_total, channels, block_cells)[slot]
    points = lax.map(gather_group, (grouped(mine, group), grouped_cell_lists, weight_groups))
    points = points.reshape(block_count, channels, block_points)
    return points.transpose(1, 0, 2).reshape(channels, block_count * block_points)


def solution(mesh):
    return jax.shard_map(
        body,
        mesh=mesh,
        in_specs=(
            P(None, ("row", "col")),
            P(None, ("row", "col")),
            P(("row", "col")),
            P(("row", "col"), None),
            P(("row", "col")),
            P("col", "row", None, None, None),
            P(),
            P(),
            P(),
            P(),
        ),
        out_specs=P(None, ("row", "col")),
        check_vma=False,
    )
```

profile of v0, /device:TPU:0, one launch (start us, length us, event | category | flops | bytes accessed | tf_op | source)
XLA Modules:
  0.0 1972.6 jit_solution(16668967088138158100)
XLA Ops:
  14.1 64.1 %while.20 = (s32[]{:T(128)}, bf16[16,8,16,512]{3,2,1,0:T(8,128)(2,1)S(1)}, bf16[16,8,16,128]{3,1,0,2:T(8,128)(2,1)S(1)}, s32[16,8,8,128]{3,2,1,0:T(8,128)S(1)}, bf16[16,8,8,128]{3,2,1,0:T(8,128)(2,1)}, /*index=5*/s32[]{:T(128)}) while((s32[]{:T(128)}, bf16[16,8,16,512]{3,2,1,0:T(8,128)(2,1)S(1)}, bf16[16,8,16,128]{3,1,0,2:T(8,128)(2,1)S(1)}, ...), condition=%wide.region_5.6_spmd, body=%wide.region_3.5_spmd.sunk | while | flops 33030144 | bytes 2474069 | solution.py:161
  97.2 93.9 %all-to-all-done.1 = bf16[32,8,16,512]{3,1,2,0:T(8,128)(2,1)} async-done(((bf16[32,8,16,512]{3,1,2,0:T(8,128)(2,1)}), bf16[32,8,16,512]{3,1,2,0:T(8,128)(2,1)}, u32[]{:S(2)}, u32[]{:S(2)}) %all-to-all-start.1) | async-done | bytes 4194336 | tf_op jit(solution)/shard_map/all_to_all | solution.py:168
  191.1 10.2 convolution_convert_fusion.2
  201.3 21.6 %copy.324 = bf16[1024,16,512]{0,2,1:T(8,128)(2,1)} copy(bf16[1024,16,512]{2,0,1:T(8,128)(2,1)} %convolution_convert_fusion.2) | data formatting | bytes 33554432 | tf_op jit(solution)/shard_map/convert_element_type | solution.py:177
  223.0 88.1 %reshape.724 = bf16[8,4,32,16,8,8,8]{2,1,0,6,5,4,3:T(4,128)(2,1)} reshape(bf16[1024,16,512]{0,2,1:T(8,128)(2,1)} %copy.324) | data formatting | bytes 33554432 | tf_op jit(solution)/shard_map/reshape | solution.py:178
  311.1 189.1 %copy.325 = bf16[16,8,8,4,8,32,8]{0,6,5,4,3,2,1:T(8,128)(2,1)} copy(bf16[16,8,8,4,8,32,8]{5,3,1,6,4,2,0:T(4,128)(2,1)} %bitcast.30) | data formatting | bytes 33554432 | tf_op jit(solution)/shard_map/transpose | solution.py:179
  500.2 50.8 %convert_bitcast_fusion.2 = bf16[128,32,16,64]{0,2,1,3:T(8,128)(2,1)} fusion(bf16[16,64,32,256]{0,3,2,1:T(8,128)(2,1)} %bitcast.31, bf16[256,128]{0,1:T(8,128)(2,1)S(1)} %convert_element_type.200), kind=kOutput, calls=%fused_computation.48 | convolution fusion | flops 2151677952 | bytes 25231360 | tf_op jit(solution)/shard_map/cxyz,zq->cxyq/dot_general | solution.py:182
  551.0 16.3 copy.329
  567.3 12.4 copy.330
  585.8 11.5 convert_element_type.209
  597.2 171.1 %all-to-all-done.2 = bf16[128,32,1024]{2,1,0:T(8,128)(2,1)} async-done(((bf16[128,32,1024]{2,1,0:T(8,128)(2,1)}), bf16[128,32,1024]{2,1,0:T(8,128)(2,1)}, u32[]{:S(2)}, u32[]{:S(2)}) %all-to-all-start.2) | async-done | bytes 8388640 | tf_op jit(solution)/shard_map/all_to_all | solution.py:186
  801.0 29.4 %fusion.100 = (f32[8,16,16,16,64]{4,3,2,1,0:T(8,128)}, f32[8,16,16,16,64]{4,3,2,1,0:T(8,128)}, f32[8,16,16,16,64]{4,3,2,1,0:T(8,128)}) fusion(bf16[8,16,16,16,128]{4,3,2,1,0:T(8,128)(2,1)} %param.19, f32[8,16,16,16,128]{4,3,2,1,0:T(8,128)} %convert_element_type.209), kind=kLoop, calls=%fused_computation.189 | loop fusion | flops 2097152 | bytes 50331648 | tf_op jit(solution)/shard_map/slice | solution.py:105
  834.9 9.6 copy.335
  851.8 25.9 %fusion.25 = bf16[8,16,16,128]{3,2,1,0:T(8,128)(2,1)S(1)} fusion(f32[8,16,16,16,64]{4,3,2,1,0:T(8,128)} %get-tuple-element.127, f32[8,16,16,16,64]{4,3,2,1,0:T(8,128)} %get-tuple-element.126, f32[8,16,16,16,64]{4,3,2,1,0:T(8,128)} %get-tuple-element.144, f32[8,16,16,128]{3,2,1,0:T(8,128)S(1)} %pad_maximum_fusion, f32[8,16,16,128]{3,2,1,0:T(8,128)S(1)} %fusion.36), kind=kLoop, calls=%fused_computation.40 | loop fusion | flops 24903680 | bytes 27787264 | tf_op jit(solution)/shard_map/reduce_sum | solution.py:107
  878.8 13.9 copy.338
  892.6 10.6 reshape.791
  907.4 25.5 %all-to-all-done.4 = bf16[4,2,131072]{2,1,0:T(2,128)(2,1)S(1)} async-done(((bf16[4,2,131072]{2,1,0:T(2,128)(2,1)}), bf16[4,2,131072]{2,1,0:T(2,128)(2,1)S(1)}, u32[]{:S(2)}, u32[]{:S(2)}) %all-to-all-start.4) | async-done | bytes 2097184 | tf_op jit(solution)/shard_map/all_to_all | solution.py:208
  938.5 15.2 copy.372
  977.9 11.3 copy.343
  996.4 57.2 %fusion.86 = f32[64,32,256,16]{2,3,1,0:T(8,128)} fusion(bf16[16,64,32,256]{0,3,2,1:T(8,128)(2,1)} %bitcast.31, bf16[16,16]{1,0:T(8,128)(2,1)S(1)} %copy-done), kind=kOutput, calls=%fused_computation.154 | convolution fusion | flops 268435456 | bytes 50332160 | tf_op jit(solution)/shard_map/oi,ixyz->oxyz/dot_general | solution.py:219
  1053.6 124.0 %all-to-all-done.5 = bf16[16,256,1024]{2,0,1:T(8,128)(2,1)} async-done(((bf16[16,256,1024]{2,0,1:T(8,128)(2,1)}), bf16[16,256,1024]{2,0,1:T(8,128)(2,1)}, u32[]{:S(2)}, u32[]{:S(2)}) %all-to-all-start.5) | async-done | bytes 8388640 | tf_op jit(solution)/shard_map/all_to_all | solution.py:216
  1177.6 12.0 copy.386
  1189.6 22.1 %reshape.733 = bf16[128,32,16,64]{3,2,1,0:T(8,128)(2,1)} reshape(bf16[8,16,32,1024]{3,2,1,0:T(8,128)(2,1)} %bitcast.233) | data formatting | bytes 16777216 | tf_op jit(solution)/shard_map/reshape | solution.py:217
  1211.7 27.8 %copy.345 = bf16[128,32,16,64]{0,2,1,3:T(8,128)(2,1)} copy(bf16[128,32,16,64]{3,2,1,0:T(8,128)(2,1)} %reshape.733) | data formatting | bytes 16777216 | tf_op jit(solution)/shard_map/reshape | solution.py:217
  1239.5 19.0 fusion.30
  1258.5 66.4 %convert_bitcast_fusion = bf16[16,64,32,256]{3,0,2,1:T(8,128)(2,1)} fusion(f32[64]{0:T(128)S(1)} %copy-done.9, f32[16,64,32,256]{3,0,2,1:T(8,128)} %fusion.30, f32[64,32,256,16]{2,3,1,0:T(8,128)} %fusion.86, bf16[16,64]{1,0:T(8,128)(2,1)S(1)} %copy-done.7, bf16[64,16]{0,1:T(8,128)(2,1)S(1)} %copy-done.8), kind=kOutput, calls=%fused_computation.42 | convolution fusion | flops 2508193792 | bytes 83890432 | tf_op jit(solution)/shard_map/oh,hxyz->oxyz/dot_general | solution.py:228
  1324.9 91.0 %copy.348 = bf16[16,64,32,256]{0,3,2,1:T(8,128)(2,1)} copy(bf16[16,64,32,256]{3,0,2,1:T(8,128)(2,1)} %convert_bitcast_fusion) | data formatting | bytes 33554432 | tf_op jit(solution)/shard_map/convert_element_type | solution.py:230
  1415.9 206.1 %copy.349 = bf16[8,4,32,16,8,8,8]{2,1,0,6,5,4,3:T(4,128)(2,1)} copy(bf16[8,4,32,16,8,8,8]{3,6,2,5,1,4,0:T(8,128)(2,1)} %bitcast.73) | data formatting | bytes 33554432 | tf_op jit(solution)/shard_map/transpose | solution.py:234
  1621.9 121.8 %reshape.735 = bf16[1024,16,512]{0,2,1:T(8,128)(2,1)} reshape(bf16[8,4,32,16,8,8,8]{2,1,0,6,5,4,3:T(4,128)(2,1)} %copy.349) | data formatting | bytes 33554432 | tf_op jit(solution)/shard_map/reshape | solution.py:234
  1743.7 23.9 %copy.351 = bf16[1024,16,512]{2,1,0:T(8,128)(2,1)} copy(bf16[1024,16,512]{0,2,1:T(8,128)(2,1)} %reshape.735) | data formatting | bytes 33554432 | tf_op jit(solution)/shard_map/reshape | solution.py:234
  1788.7 95.1 %all-to-all-done.6 = bf16[32,8,16,512]{3,1,2,0:T(8,128)(2,1)} async-done(((bf16[32,8,16,512]{3,1,2,0:T(8,128)(2,1)}), bf16[32,8,16,512]{3,1,2,0:T(8,128)(2,1)}, u32[]{:S(2)}, u32[]{:S(2)}) %all-to-all-start.6) | async-done | bytes 4194336 | tf_op jit(solution)/shard_map/all_to_all | solution.py:242
  1892.7 78.2 %while.21 = (s32[]{:T(128)}, bf16[16,8,16,128]{3,2,1,0:T(8,128)(2,1)S(1)}, bf16[16,8,16,512]{3,2,1,0:T(8,128)(2,1)S(1)}, s32[16,8,8,128]{3,2,1,0:T(8,128)}, bf16[16,8,8,128]{3,2,1,0:T(8,128)(2,1)}, /*index=5*/s32[]{:T(128)}) while((s32[]{:T(128)}, bf16[16,8,16,128]{3,2,1,0:T(8,128)(2,1)S(1)}, bf16[16,8,16,512]{3,2,1,0:T(8,128)(2,1)S(1)}, ...), condition=%wide.region_9.10_spmd, body=%wide.region_7.9_spmd.sunk | while | flops 33030144 | bytes 2409549 | solution.py:244
  (257 shorter events, 298.4 us)
Async XLA Ops:
  0.0 996.4 %copy-start = (bf16[16,16]{1,0:T(8,128)(2,1)S(1)}, bf16[16,16]{1,0:T(8,128)(2,1)}, u32[]{:S(2)}) copy-start(bf16[16,16]{1,0:T(8,128)(2,1)} %param.20) | copy-start | bytes 1540
  0.9 0.9 copy-start.11
  4.4 85.4 %all-to-all-start = ((s32[32,1,8]{2,1,0:T(1,128)}), s32[32,1,8]{2,1,0:T(1,128)S(1)}, u32[]{:S(2)}, u32[]{:S(2)}) async-start(s32[32,1,8]{2,1,0:T(1,128)} %bitcast.11), calls=%async_computation | async-start | bytes 32768 | tf_op jit(solution)/shard_map/all_to_all | solution.py:169
  78.3 5.3 copy-start.2
  89.8 101.3 %all-to-all-start.1 = ((bf16[32,8,16,512]{3,1,2,0:T(8,128)(2,1)}), bf16[32,8,16,512]{3,1,2,0:T(8,128)(2,1)}, u32[]{:S(2)}, u32[]{:S(2)}) async-start(bf16[32,8,16,512]{3,1,2,0:T(8,128)(2,1)} %copy.322), calls=%async_computation.1 | async-start | bytes 8388608 | tf_op jit(solution)/shard_map/all_to_all | solution.py:168
  96.5 0.6 copy-start.3
  579.7 188.6 %all-to-all-start.2 = ((bf16[128,32,1024]{2,1,0:T(8,128)(2,1)}), bf16[128,32,1024]{2,1,0:T(8,128)(2,1)}, u32[]{:S(2)}, u32[]{:S(2)}) async-start(bf16[128,32,1024]{2,1,0:T(8,128)(2,1)} %copy.330), calls=%async_computation.2 | async-start | bytes 16777216 | tf_op jit(solution)/shard_map/all_to_all | solution.py:186
  797.3 33.6 %all-to-all-start.3 = ((bf16[4,2,131072]{2,1,0:T(2,128)(2,1)}), bf16[4,2,131072]{2,1,0:T(2,128)(2,1)S(1)}, u32[]{:S(2)}, u32[]{:S(2)}) async-start(bf16[4,2,131072]{2,1,0:T(2,128)(2,1)} %reshape.789), calls=%async_computation.3 | async-start | bytes 4194304 | tf_op jit(solution)/shard_map/all_to_all | solution.py:195
  903.2 29.7 %all-to-all-start.4 = ((bf16[4,2,131072]{2,1,0:T(2,128)(2,1)}), bf16[4,2,131072]{2,1,0:T(2,128)(2,1)S(1)}, u32[]{:S(2)}, u32[]{:S(2)}) async-start(bf16[4,2,131072]{2,1,0:T(2,128)(2,1)} %reshape.791), calls=%async_computation.4 | async-start | bytes 4194304 | tf_op jit(solution)/shard_map/all_to_all | solution.py:208
  989.2 5.7 copy-start.6
  989.2 5.9 copy-start.4
  989.2 188.4 %all-to-all-start.5 = ((bf16[16,256,1024]{2,0,1:T(8,128)(2,1)}), bf16[16,256,1024]{2,0,1:T(8,128)(2,1)}, u32[]{:S(2)}, u32[]{:S(2)}) async-start(bf16[16,256,1024]{2,0,1:T(8,128)(2,1)} %copy.343), calls=%async_computation.5 | async-start | bytes 16777216 | tf_op jit(solution)/shard_map/all_to_all | solution.py:216
  1239.5 19.0 copy-start.7
  1239.5 19.0 copy-start.8
  1239.5 19.0 copy-start.9
  1767.6 8.7 copy-start.5
  1778.8 9.9 copy-start.10
  1778.8 9.9 copy-start.12
  1785.1 98.7 %all-to-all-start.6 = ((bf16[32,8,16,512]{3,1,2,0:T(8,128)(2,1)}), bf16[32,8,16,512]{3,1,2,0:T(8,128)(2,1)}, u32[]{:S(2)}, u32[]{:S(2)}) async-start(bf16[32,8,16,512]{3,1,2,0:T(8,128)(2,1)} %copy.352), calls=%async_computation.6 | async-start | bytes 8388608 | tf_op jit(solution)/shard_map/all_to_all | solution.py:242
  1889.8 82.3 %copy-start.1 = (bf16[16,16]{1,0:T(8,128)(2,1)S(1)}, bf16[16,16]{1,0:T(8,128)(2,1)}, u32[]{:S(2)}) copy-start(bf16[16,16]{1,0:T(8,128)(2,1)} %param.20) | copy-start | bytes 1540
where the time goes:
time: 2000 us; the launch traced here: 1970 us
  local copies, waits for them, and re-layouts  1030 us (52%)
  waiting for transfers between devices  509 us (25%)
  matrix products  225 us (11%)
  other arithmetic  173 us (9%)
  starting transfers between devices  35.5 us (2%)
    transpose x1, local copies, waits for them, and re-layouts, body(): layer_grid.transpose(1, 3, 5, 0, 2, 4, 6)  206 us
    transpose x1, local copies, waits for them, and re-layouts, body(): field.transpose(3, 0, 4, 1, 5, 2, 6)  189 us
    all_to_all x1, waiting for transfers between devices, body(): lax.all_to_all(zspec, 'col', split_axis=0, concat_axis=1, tiled=True)  171 us
    reshape x2, local copies, waits for them, and re-layouts, body(): layer_grid.transpose(1, 3, 5, 0, 2, 4, 6)  146 us
    all_to_all x1, waiting for transfers between devices, body(): yinv = lax.all_to_all(yinv, 'col', split_axis=1, concat_axis=0, tiled=True)  124 us
    all_to_all x1, waiting for transfers between devices, body(): lax.all_to_all(owned_vals, ('row', 'col'), split_axis=0, concat_axis=0, t...  95.1 us
    all_to_all x1, waiting for transfers between devices, body(): lax.all_to_all(send_vals, ('row', 'col'), split_axis=0, concat_axis=0, ti...  93.9 us
    convert_element_type x1, local copies, waits for them, and re-layouts, body(): layer_field = jnp.einsum('oh,hxyz->oxyz', mlp_out, hidden, preferred_elem...  91 us
  transfers between devices with their start and end apart: 7, of which 5 were waited for; matrix products, arithmetic and copies ran while one was open for 9% of the time, Pallas kernels for 0%

commit v1 on v0

v1 whole, which is shorter than its diff:
```python
import functools
import math

import jax
import jax.numpy as jnp
from jax import lax
from jax.experimental import pallas as pl
from jax.experimental.pallas import tpu as pltpu
from jax.sharding import PartitionSpec as P

GRID = 256
BE = 8
PB_PTS = 128


def frequencies(count, length):
    index = jnp.arange(count, dtype=jnp.int32)
    return jnp.where(index < count // 2, index, length - count + index)


def angles(length, freq):
    places = jnp.arange(length, dtype=jnp.int32)
    turns = places[:, None] * freq[None, :] % length
    return 2.0 * math.pi / length * turns.astype(jnp.float32)


def forward_tables(length, count):
    factor = 1.0 / math.sqrt(length)
    theta = angles(length, jnp.arange(count, dtype=jnp.int32))
    real_basis_table = jnp.stack([jnp.cos(theta) * factor, -jnp.sin(theta) * factor], -1).reshape(
        length, 2 * count
    )
    theta = angles(length, frequencies(count, length))
    cosine = jnp.cos(theta) * factor
    sine = jnp.sin(theta) * factor
    from_real = jnp.stack([cosine, -sine], -1)
    from_imag = jnp.stack([sine, cosine], -1)
    paired = jnp.stack([from_real, from_imag], 0)
    planar = jnp.swapaxes(paired, 2, 3)
    return (
        real_basis_table.astype(jnp.bfloat16),
        paired.reshape(2, length, 2 * count).astype(jnp.bfloat16),
        planar.reshape(2, length, 2 * count).astype(jnp.bfloat16),
    )


def inverse_tables(length, count):
    factor = 1.0 / math.sqrt(length)
    theta = angles(length, frequencies(count, length)).T
    cosine = jnp.cos(theta) * factor
    sine = jnp.sin(theta) * factor
    from_real = jnp.stack([cosine, sine], 1)
    from_imag = jnp.stack([-sine, cosine], 1)
    paired = jnp.stack([from_real, from_imag], 1)
    planar = jnp.swapaxes(paired, 0, 1)
    theta = angles(length, jnp.arange(count, dtype=jnp.int32)).T
    double = jnp.where(jnp.arange(count) == 0, 1.0, 2.0).astype(jnp.float32)[:, None]
    real_out = jnp.stack([double * jnp.cos(theta) * factor, -double * jnp.sin(theta) * factor], 1)
    return (
        real_out.reshape(2 * count, length).astype(jnp.bfloat16),
        paired.reshape(2 * count, 2, length).astype(jnp.bfloat16),
        planar.reshape(2 * count, 2, length).astype(jnp.bfloat16),
    )


BF = jnp.bfloat16
F32 = jnp.float32
CORNERS = 8
VMEM_BYTES = 48 * 1024 * 1024


def vmem(limit=VMEM_BYTES):
    return pltpu.CompilerParams(vmem_limit_bytes=limit)


def block_masks(rows, channels):
    edge = BE
    base = channels + CORNERS
    vx, vy, vz = rows[base : base + 1], rows[base + 1 : base + 2], rows[base + 2 : base + 3]
    place = lax.broadcasted_iota(jnp.int32, (edge, PB_PTS), 0).astype(F32)
    plane = lax.broadcasted_iota(jnp.int32, (edge, edge, PB_PTS), 0).astype(F32)
    z_low, z_high = place == vz, place == vz + 1.0
    y_low, y_high = plane == vy[None], plane == (vy + 1.0)[None]
    parts = []
    for dx in range(2):
        lines = []
        for dy in range(2):
            k = channels + dx * 4 + dy * 2
            lines.append(
                jnp.where(z_low, rows[k : k + 1], jnp.where(z_high, rows[k + 1 : k + 2], 0.0))
            )
        face = jnp.where(y_low, lines[0][None], jnp.where(y_high, lines[1][None], 0.0))
        parts.append(face.reshape(edge * edge, PB_PTS))
    spread = jnp.concatenate(parts, axis=1).astype(BF)
    return spread, place == vx, place == vx + 1.0


def spread_kernel(channels, recv_ref, out_ref):
    for s in range(recv_ref.shape[0]):
        rows = recv_ref[s].astype(F32)
        spread, x_low, x_high = block_masks(rows, channels)
        feats = rows[:channels][:, None, :]
        low = jnp.where(x_low[None], feats, 0.0).reshape(channels * BE, PB_PTS)
        high = jnp.where(x_high[None], feats, 0.0).reshape(channels * BE, PB_PTS)
        both = jnp.concatenate([low, high], axis=1).astype(BF)
        out_ref[s] = lax.dot_general(
            spread, both, (((1,), (1,)), ((), ())), preferred_element_type=F32
        ).astype(BF)


def land_kernel(
    y_blocks, x_blocks, z_blocks, id_row, id_col, blocks_ref, table_ref, out_ref, own_ref, land, grid
):
    slots = id_row.shape[1]
    local = land.shape[0]
    lanes = blocks_ref.shape[-1]
    parts = out_ref.shape[0]

    @pl.when(pl.program_id(0) == 0)
    def _():
        cells = lax.broadcasted_iota(jnp.int32, (local, slots), 0) + 1
        land[...] = jnp.where(cells == id_row[...], 1.0, 0.0).astype(BF)

    same = jnp.where(id_col[...] == id_row[...], 1.0, 0.0).astype(BF)
    for dz in range(BE):
        piece = blocks_ref[0, dz]
        grid[dz] = jnp.dot(land[...], piece, preferred_element_type=F32).astype(BF)
        own_ref[0, dz] = jnp.dot(same, piece, preferred_element_type=F32).astype(BF)
    for bx in range(x_blocks):
        for by in range(y_blocks):
            start = (bx * y_blocks + by) * z_blocks
            column = grid[:, start : start + z_blocks, :].reshape(BE * z_blocks, lanes)
            got = jnp.dot(table_ref[...], column, preferred_element_type=F32).astype(BF)
            out_ref[:, by, 0, :, bx * lanes : (bx + 1) * lanes] = got.reshape(
                parts, got.shape[0] // parts, lanes
            )


def mix_kernel(spec_ref, weight_ref, out_ref):
    half = spec_ref.shape[-1] // 2
    channels = spec_ref.shape[2]
    first = lax.broadcasted_iota(jnp.int32, weight_ref.shape[-2:], 1) < half

    def step(j, carry):
        value = spec_ref[0, pl.ds(j, 1)][0]
        turned = pltpu.roll(value, half, 1)
        total = jnp.zeros(weight_ref.shape[-2:], F32)
        for c in range(channels):
            w = weight_ref[0, pl.ds(j, 1), c][0].astype(F32)
            other = pltpu.roll(w, half, 1)
            real = jnp.where(first, w, other)
            imag = jnp.where(first, -other, w)
            total = total + value[c : c + 1] * real + turned[c : c + 1] * imag
        out_ref[0, pl.ds(j, 1)] = total.astype(BF)[None]
        return carry

    lax.fori_loop(0, spec_ref.shape[1], step, 0)


def back_kernel(z_blocks, in_ref, table_ref, out_ref):
    lanes = out_ref.shape[-1]
    for dy in range(BE):
        modes = in_ref[:, dy, :, :].reshape(table_ref.shape[1], lanes)
        got = jnp.dot(table_ref[...], modes, preferred_element_type=F32)
        out_ref[0, :, dy * BE : (dy + 1) * BE, :] = got.reshape(z_blocks, BE, lanes)


def point_kernel(channels, recv_ref, spec_ref, own_ref, skip_ref, in_ref, bias_ref, last_ref, out_ref):
    group, cells, lanes = spec_ref.shape
    own = own_ref[...].reshape(group * cells, lanes)
    pre = spec_ref[...].reshape(group * cells, lanes) + jnp.dot(
        own, skip_ref[...], preferred_element_type=F32
    )
    hidden = jnp.dot(pre.astype(BF), in_ref[...], preferred_element_type=F32) + bias_ref[...]
    hidden = jax.nn.gelu(hidden, approximate=True).astype(BF)
    layer = jnp.dot(hidden, last_ref[...], preferred_element_type=F32).astype(BF)
    layer = layer.reshape(group, cells, lanes)
    for s in range(group):
        rows = recv_ref[s].astype(F32)
        spread, x_low, x_high = block_masks(rows, channels)
        picked = lax.dot_general(
            layer[s], spread, (((0,), (0,)), ((), ())), preferred_element_type=F32
        )
        low = picked[:, :PB_PTS].reshape(channels, BE, PB_PTS)
        high = picked[:, PB_PTS:].reshape(channels, BE, PB_PTS)
        total = jnp.where(x_low[None], low, 0.0) + jnp.where(x_high[None], high, 0.0)
        out_ref[s] = jnp.sum(total, axis=1).astype(BF)


def whole_spec(shape):
    return pl.BlockSpec(shape, lambda *_: (0,) * len(shape))


def body(
    features,
    point_weights,
    point_corner,
    block_owner,
    block_cell,
    spec_weight,
    skip_weight,
    mlp_in,
    mlp_bias,
    mlp_out,
):
    row_count = lax.axis_size("row")
    col_count = lax.axis_size("col")
    devices = row_count * col_count
    channels = features.shape[0]
    block_count = block_cell.shape[0]
    edge_len = BE
    cells = edge_len * edge_len
    lanes = channels * edge_len
    grid_len = GRID
    mode_count = spec_weight.shape[-1] // 2
    hid = mlp_in.shape[0]
    capacity = max(2, (2 * block_count + devices - 1) // devices)
    slots = devices * capacity
    x_local = grid_len // row_count
    y_local = grid_len // col_count
    x_blocks = x_local // edge_len
    y_blocks = y_local // edge_len
    z_blocks = grid_len // edge_len
    local_blocks = x_blocks * y_blocks * z_blocks
    wide = x_blocks * lanes
    owner = block_owner[:, 0]
    block_ids = jnp.arange(block_count, dtype=jnp.int32)
    earlier = block_ids[None, :] < block_ids[:, None]
    rank = jnp.sum((owner[None, :] == owner[:, None]) & earlier, axis=1)
    slot = owner * capacity + rank
    slot_ids = jnp.arange(slots, dtype=jnp.int32)
    match = slot[None, :] == slot_ids[:, None]
    filled = jnp.any(match, axis=1)
    block_of_slot = jnp.sum(jnp.where(match, block_ids[None, :], 0), axis=1)
    interior = edge_len - 1
    corner = point_corner.reshape(block_count, PB_PTS)
    code = (block_cell + 1)[:, None] + jnp.zeros((1, PB_PTS), jnp.int32)
    extra = [
        corner // (interior * interior),
        corner // interior % interior,
        corner % interior,
        code // 32,
        code % 32,
    ]
    used = channels + CORNERS + len(extra)
    rows_sent = (used + 15) // 16 * 16
    extra = extra + [jnp.zeros_like(corner)] * (rows_sent - used)
    payload = jnp.concatenate(
        [
            features.reshape(channels, block_count, PB_PTS),
            point_weights.reshape(CORNERS, block_count, PB_PTS),
            jnp.stack(extra, 0).astype(BF),
        ],
        axis=0,
    ).transpose(1, 0, 2)
    sent = jnp.where(filled[:, None, None], payload[block_of_slot], jnp.zeros((), BF))
    recv = lax.all_to_all(sent, ("row", "col"), split_axis=0, concat_axis=0, tiled=True)
    id_at = channels + CORNERS + 3
    ids = recv[:, id_at, 0].astype(jnp.int32) * 32 + recv[:, id_at + 1, 0].astype(jnp.int32)
    group = 8
    recv_spec = pl.BlockSpec((group, rows_sent, PB_PTS), lambda g: (g, 0, 0))
    cell_spec = pl.BlockSpec((group, cells, lanes), lambda g: (g, 0, 0))
    blocks = pl.pallas_call(
        functools.partial(spread_kernel, channels),
        out_shape=jax.ShapeDtypeStruct((slots, cells, lanes), BF),
        grid=(slots // group,),
        in_specs=[recv_spec],
        out_specs=cell_spec,
        compiler_params=vmem(),
        name="spread",
    )(recv)
    by_cell = blocks.transpose(1, 0, 2).reshape(edge_len, edge_len, slots, lanes)
    table_z, table_y, table_x = forward_tables(grid_len, mode_count)
    inv_z, inv_y, inv_x = inverse_tables(grid_len, mode_count)
    z_table = (
        table_z.reshape(z_blocks, edge_len, 2 * mode_count)
        .transpose(2, 1, 0)
        .reshape(2 * mode_count, grid_len)
    )
    modes_out = 2 * mode_count // col_count
    zspec, own = pl.pallas_call(
        functools.partial(land_kernel, y_blocks, x_blocks, z_blocks),
        out_shape=(
            jax.ShapeDtypeStruct((col_count, y_blocks, edge_len, modes_out, wide), BF),
            jax.ShapeDtypeStruct((edge_len, edge_len, slots, lanes), BF),
        ),
        grid=(edge_len,),
        in_specs=[
            whole_spec((1, slots)),
            whole_spec((slots, 1)),
            pl.BlockSpec((1, edge_len, slots, lanes), lambda d: (d, 0, 0, 0)),
            whole_spec((2 * mode_count, grid_len)),
        ],
        out_specs=(
            pl.BlockSpec((col_count, y_blocks, 1, modes_out, wide), lambda d: (0, 0, d, 0, 0)),
            pl.BlockSpec((1, edge_len, slots, lanes), lambda d: (d, 0, 0, 0)),
        ),
        scratch_shapes=[
            pltpu.VMEM((local_blocks, slots), BF),
            pltpu.VMEM((edge_len, local_blocks, lanes), BF),
        ],
        compiler_params=vmem(),
        name="land",
    )(ids[None, :], ids[:, None], by_cell, z_table)
    own = own.reshape(cells, slots, lanes).transpose(1, 0, 2)
    zspec = lax.all_to_all(zspec, "col", split_axis=0, concat_axis=0, tiled=True)
    kz_local = modes_out // 2
    zspec = zspec.reshape(grid_len, modes_out, wide).transpose(1, 0, 2)
    yspec = jnp.einsum(
        "krn,rq->kqn",
        zspec.reshape(kz_local, 2 * grid_len, wide),
        table_y.reshape(2 * grid_len, 2 * mode_count),
        preferred_element_type=F32,
    ).astype(BF)
    spots = jnp.arange(wide, dtype=jnp.int32)
    channel = spots // edge_len % channels
    target = channel * x_local + spots // lanes * edge_len + spots % edge_len
    order = (target[:, None] == spots[None, :]).astype(BF)
    yspec = jnp.einsum("kqn,nm->kqm", yspec, order, preferred_element_type=F32).astype(BF)
    yspec = yspec.reshape(kz_local, 2 * mode_count, channels, x_local)
    yspec = lax.all_to_all(yspec, "row", split_axis=1, concat_axis=3, tiled=True)
    ky_local = yspec.shape[1] // 2
    spectrum = jnp.einsum(
        "kjpcx,pxq->kjcq",
        yspec.reshape(kz_local, ky_local, 2, channels, grid_len),
        table_x,
        preferred_element_type=F32,
    ).astype(BF).astype(F32)
    mode_spec = pl.BlockSpec((1, ky_local, channels, 2 * mode_count), lambda k: (k, 0, 0, 0))
    mixed = pl.pallas_call(
        mix_kernel,
        out_shape=jax.ShapeDtypeStruct(spectrum.shape, BF),
        grid=(kz_local,),
        in_specs=[
            mode_spec,
            pl.BlockSpec((1,) + spec_weight.shape[1:], lambda k: (k, 0, 0, 0, 0)),
        ],
        out_specs=mode_spec,
        compiler_params=vmem(),
        name="mix",
    )(spectrum, spec_weight)
    xinv = jnp.einsum("kjoq,qpx->kjpox", mixed, inv_x, preferred_element_type=F32).astype(BF)
    xinv = xinv.reshape(kz_local, 2 * ky_local, channels, grid_len)
    xinv = lax.all_to_all(xinv, "row", split_axis=3, concat_axis=1, tiled=True)
    xinv = xinv.reshape(kz_local, 2 * mode_count, wide)
    xinv = jnp.einsum("kqm,nm->kqn", xinv, order, preferred_element_type=F32).astype(BF)
    yinv = jnp.einsum(
        "rq,kqn->krn",
        inv_y.reshape(2 * mode_count, 2 * grid_len).T,
        xinv,
        preferred_element_type=F32,
    ).astype(BF)
    yinv = yinv.reshape(modes_out, grid_len, wide).transpose(1, 0, 2)
    yinv = lax.all_to_all(yinv, "col", split_axis=0, concat_axis=0, tiled=True)
    yinv = yinv.reshape(col_count, y_local, modes_out, wide)
    spectral = pl.pallas_call(
        functools.partial(back_kernel, z_blocks),
        out_shape=jax.ShapeDtypeStruct((x_blocks * y_blocks, z_blocks, cells, lanes), F32),
        grid=(x_blocks, y_blocks),
        in_specs=[
            pl.BlockSpec(
                (col_count, edge_len, modes_out, lanes), lambda bx, by: (0, by, 0, bx)
            ),
            whole_spec((grid_len, 2 * mode_count)),
        ],
        out_specs=pl.BlockSpec(
            (1, z_blocks, cells, lanes), lambda bx, by: (bx * y_blocks + by, 0, 0, 0)
        ),
        compiler_params=vmem(),
        name="back",
    )(yinv, inv_z.T)
    spectral = spectral.reshape(local_blocks, cells, lanes)[jnp.maximum(ids - 1, 0)]
    eye = jnp.eye(edge_len, dtype=BF)
    values = pl.pallas_call(
        functools.partial(point_kernel, channels),
        out_shape=jax.ShapeDtypeStruct((slots, channels, PB_PTS), BF),
        grid=(slots // group,),
        in_specs=[
            recv_spec,
            cell_spec,
            cell_spec,
            whole_spec((lanes, lanes)),
            whole_spec((lanes, hid * edge_len)),
            whole_spec((1, hid * edge_len)),
            whole_spec((hid * edge_len, lanes)),
        ],
        out_specs=pl.BlockSpec((group, channels, PB_PTS), lambda g: (g, 0, 0)),
        compiler_params=vmem(),
        name="points",
    )(
        recv,
        spectral,
        own,
        jnp.kron(skip_weight.T, eye),
        jnp.kron(mlp_in.T, eye),
        jnp.repeat(mlp_bias, edge_len)[None, :],
        jnp.kron(mlp_out.T, eye),
    )
    returned = lax.all_to_all(values, ("row", "col"), split_axis=0, concat_axis=0, tiled=True)
    points = returned[slot]
    return points.transpose(1, 0, 2).reshape(channels, block_count * PB_PTS)


def solution(mesh):
    return jax.shard_map(
        body,
        mesh=mesh,
        in_specs=(
            P(None, ("row", "col")),
            P(None, ("row", "col")),
            P(("row", "col")),
            P(("row", "col"), None),
            P(("row", "col")),
            P("col", "row", None, None, None),
            P(),
            P(),
            P(),
            P(),
        ),
        out_specs=P(None, ("row", "col")),
        check_vma=False,
    )
```

time: 2000 us -> 831 us (0.42); the launches traced: 1970 us -> 826 us
  local copies, waits for them, and re-layouts: 1030 us -> 169 us
  matrix products: 225 us -> 19.9 us
  other arithmetic: 173 us -> 19.8 us
  Pallas kernels: 0 us -> 115 us
  waiting for transfers between devices: 509 us -> 469 us
    transpose x2 -> x4, local copies, waits for them, and re-layouts: 395 us -> 9.5 us  [the longest x1 6.85 us: body(): blocks.transpose(1, 0, 2).reshape(edge_len, edge_len, slots, lanes)]
    reshape x9 -> x6, local copies, waits for them, and re-layouts: 313 us -> 30.2 us  [the longest x1 11.3 us: body(): zspec = zspec.reshape(grid_len, modes_out, wide).transpose(1, 0, 2)]
    dot_general x40 -> x3, matrix products: 225 us -> 17.6 us  [the longest x1 8.48 us: body(): jnp.einsum('rq,kqn->krn', inv_y.reshape(2 * mode_count, 2 * grid_len).T,...]
    convert_element_type x7 -> x2, local copies, waits for them, and re-layouts: 140 us -> 5.6 us  [the longest x1 3.92 us: body(): jnp.einsum('kqn,nm->kqm', yspec, order, preferred_element_type=F32)]
    reduce_sum x33 -> x0, other arithmetic: 122 us -> none  [the longest x16 47.9 us: spread_point_group(): jnp.einsum('eqf,esfx->eqx', feature_rows, basis_table, preferred_element_...]
    pallas_call x0 -> x5, Pallas kernels: none -> 115 us  [the longest x1 37.2 us: body(): pl.pallas_call(functools.partial(point_kernel, channels), out_shape=jax.S...]
    all_to_all x5 -> x4, waiting for transfers between devices: 484 us -> 419 us  [the longest x1 182 us: body(): lax.all_to_all(zspec, 'col', split_axis=0, concat_axis=0, tiled=True)]
    slice x1 -> x0, other arithmetic: 29.4 us -> none  [mix_modes(): imag_part = jnp.concatenate([-coeffs[..., half:], coeffs[..., half:]], -1)]
  transfers between devices with their start and end apart: 7 -> 6, of which waited for: 5 -> 6; matrix products, arithmetic and copies ran while one was open for 9% -> 3% of each run, Pallas kernels for 0% -> 0%
where the time goes in v1:
time: 831 us; the launch traced here: 826 us
  waiting for transfers between devices  469 us (56%)
  local copies, waits for them, and re-layouts  169 us (20%)
  Pallas kernels  115 us (14%)
  starting transfers between devices  32.2 us (4%)
  matrix products  19.9 us (2%)
  other arithmetic  19.8 us (2%)
    all_to_all x1, waiting for transfers between devices, body(): lax.all_to_all(zspec, 'col', split_axis=0, concat_axis=0, tiled=True)  182 us
    all_to_all x1, waiting for transfers between devices, body(): yinv = lax.all_to_all(yinv, 'col', split_axis=0, concat_axis=0, tiled=True)  164 us
    all_to_all x1, waiting for transfers between devices, body(): lax.all_to_all(sent, ('row', 'col'), split_axis=0, concat_axis=0, tiled=T...  44.9 us
    pallas_call x1, Pallas kernels, body(): pl.pallas_call(functools.partial(point_kernel, channels), out_shape=jax.S...  37.2 us
    unnamed x25, local copies, waits for them, and re-layouts  32.7 us
    all_to_all x1, waiting for transfers between devices, body(): lax.all_to_all(values, ('row', 'col'), split_axis=0, concat_axis=0, tiled...  27.6 us
    pallas_call x1, Pallas kernels, body(): pl.pallas_call(functools.partial(back_kernel, z_blocks), out_shape=jax.Sh...  27.1 us
    all_to_all x1, waiting for transfers between devices, body(): xinv = lax.all_to_all(xinv, 'row', split_axis=3, concat_axis=1, tiled=True)  25.6 us
  transfers between devices with their start and end apart: 6, of which 6 were waited for; matrix products, arithmetic and copies ran while one was open for 3% of the time, Pallas kernels for 0%

profile of v1, /device:TPU:0, one launch (start us, length us, event | category | flops | bytes accessed | tf_op | source)
XLA Modules:
  0.0 825.6 jit_solution(10651134229569091213)
XLA Ops:
  13.9 7.5 all-to-all-start
  26.6 44.9 %all-to-all-done.recv_ref = bf16[256,32,128]{2,1,0:T(8,128)(2,1)S(1)} async-done(((bf16[256,32,128]{2,1,0:T(8,128)(2,1)}), bf16[256,32,128]{2,1,0:T(8,128)(2,1)S(1)}, u32[]{:S(2)}, u32[]{:S(2)}) %all-to-all-start) | async-done | bytes 2097184 | tf_op jit(solution)/shard_map/all_to_all | solution.py:257
  71.5 15.7 %spread.1 = bf16[256,64,128]{2,1,0:T(8,128)(2,1)} custom-call(bf16[256,32,128]{2,1,0:T(8,128)(2,1)S(1)} %all-to-all-done.recv_ref), custom_call_target="tpu_custom_call" | custom-call | tf_op jit(solution)/shard_map/spread/pallas_call | solution.py:263
  87.2 6.9 copy.216
  98.7 19.3 %land.1 = (bf16[8,4,8,16,1024]{4,3,2,1,0:T(8,128)(2,1)}, bf16[8,8,256,128]{3,2,1,0:T(8,128)(2,1)S(1)}) custom-call(s32[1,256]{1,0:T(1,128)S(1)} %bitcast.144, s32[256,1]{1,0:T(8,128)S(1)} %bitcast.141, bf16[8,8,256,128]{3,2,1,0:T(8,128)(2,1)} %bitcast.151, bf16[128,256]{1,0:T(8,128)(2,1)S(1)} %copy.219.table_ref), custom_call_target="tpu_custom_call" | custom-call | tf_op jit(solution)/shard_map/land/pallas_call | solution.py:281
  120.0 5.4 all-to-all-start.1
  126.2 182.4 %all-to-all-done.1 = bf16[8,4,8,16,1024]{4,3,2,1,0:T(8,128)(2,1)} async-done(((bf16[8,4,8,16,1024]{4,3,2,1,0:T(8,128)(2,1)}), bf16[8,4,8,16,1024]{4,3,2,1,0:T(8,128)(2,1)}, u32[]{:S(2)}, u32[]{:S(2)}) %all-to-all-start.1) | async-done | bytes 8388640 | tf_op jit(solution)/shard_map/all_to_all | solution.py:306
  308.6 11.3 %copy.220 = bf16[256,16,1024]{2,0,1:T(8,128)(2,1)} copy(bf16[256,16,1024]{2,1,0:T(8,128)(2,1)} %bitcast.22) | data formatting | bytes 16777216 | tf_op jit(solution)/shard_map/reshape | solution.py:308
  319.9 8.5 %fusion.15 = bf16[8,128,1024]{2,1,0:T(8,128)(2,1)} fusion(s32[1024]{0:T(1024)S(1)} %fusion.74, bf16[512,128,1]{1,0,2:T(8,128)(2,1)S(1)} %bitcast.172, bf16[8,512,1024]{2,1,0:T(8,128)(2,1)} %bitcast.159), kind=kOutput, calls=%fused_computation.17 | convolution fusion | flops 3224371200 | bytes 10620928 | tf_op jit(solution)/shard_map/kqn,nm->kqm/dot_general | solution.py:319
  332.3 7.4 copy.223
  339.7 5.9 reshape.994
  350.7 25.3 %all-to-all-done.2 = bf16[4,2,131072]{2,1,0:T(2,128)(2,1)} async-done(((bf16[4,2,131072]{2,1,0:T(2,128)(2,1)}), bf16[4,2,131072]{2,1,0:T(2,128)(2,1)}, u32[]{:S(2)}, u32[]{:S(2)}) %all-to-all-start.2) | async-done | bytes 2097184 | tf_op jit(solution)/shard_map/all_to_all | solution.py:321
  376.0 5.8 reshape.995
  381.9 9.6 %copy.225 = bf16[8,32,16,4,64]{4,3,2,1,0:T(4,128)(2,1)} copy(bf16[8,32,16,4,64]{4,2,0,1,3:T(8,128)(2,1)} %bitcast.152) | data formatting | bytes 4194304 | tf_op jit(solution)/shard_map/all_to_all | solution.py:321
  391.4 7.0 reshape.952
  400.7 15.6 %mix.1 = bf16[8,16,16,128]{3,2,1,0:T(8,128)(2,1)S(1)} custom-call(f32[8,16,16,128]{3,2,1,0:T(8,128)S(1)} %fusion.23.spec_ref, bf16[8,16,16,16,128]{4,3,2,1,0:T(8,128)(2,1)} %weight_ref.1), custom_call_target="tpu_custom_call" | custom-call | tf_op jit(solution)/shard_map/mix/pallas_call | solution.py:330
  418.7 15.2 %copy.228 = bf16[8,32,16,256]{1,2,0,3:T(8,128)(2,1)} copy(bf16[8,32,16,256]{3,2,1,0:T(8,128)(2,1)} %bitcast.157) | data formatting | bytes 4194304 | tf_op jit(solution)/shard_map/reshape | solution.py:343
  433.9 10.6 %reshape.996 = bf16[4,2,131072]{2,1,0:T(2,128)(2,1)} reshape(bf16[256,8,16,32]{3,2,1,0:T(8,128)(2,1)} %bitcast.146) | data formatting | bytes 4194304
  444.5 4.7 all-to-all-start.3
  449.4 25.6 %all-to-all-done.3 = bf16[4,2,131072]{2,1,0:T(2,128)(2,1)} async-done(((bf16[4,2,131072]{2,1,0:T(2,128)(2,1)}), bf16[4,2,131072]{2,1,0:T(2,128)(2,1)}, u32[]{:S(2)}, u32[]{:S(2)}) %all-to-all-start.3) | async-done | bytes 2097184 | tf_op jit(solution)/shard_map/all_to_all | solution.py:344
  474.9 7.4 reshape.997
  482.3 11.9 %copy.229 = bf16[8,32,16,4,64]{4,2,1,3,0:T(8,128)(2,1)} copy(bf16[8,32,16,4,64]{1,2,0,4,3:T(8,128)(2,1)} %bitcast.147) | data formatting | bytes 4194304 | tf_op jit(solution)/shard_map/all_to_all | solution.py:344
  494.3 6.5 reshape.954
  500.8 8.5 %convolution_convert_fusion = bf16[8,1024,512]{1,2,0:T(8,128)(2,1)} fusion(bf16[8,128,1024]{2,1,0:T(8,128)(2,1)} %reshape.954, s32[1024]{0:T(1024)S(1)} %fusion.74, bf16[128,512]{1,0:T(8,128)(2,1)S(1)} %bitcast.171), kind=kOutput, calls=%fused_computation.4 | convolution fusion | flops 3227516928 | bytes 10620928 | tf_op jit(solution)/shard_map/rq,kqn->krn/dot_general | solution.py:347
  509.3 11.3 %copy.266 = bf16[16,256,1024]{2,0,1:T(8,128)(2,1)} copy(bf16[16,256,1024]{2,1,0:T(8,128)(2,1)} %bitcast.158) | data formatting | bytes 16777216 | tf_op jit(solution)/shard_map/reshape | solution.py:353
  520.6 5.4 all-to-all-start.4
  538.4 6.8 copy.267
  545.4 163.7 %all-to-all-done.4 = bf16[256,16,1024]{2,1,0:T(8,128)(2,1)} async-done(((bf16[256,16,1024]{2,1,0:T(8,128)(2,1)}), bf16[256,16,1024]{2,1,0:T(8,128)(2,1)}, u32[]{:S(2)}, u32[]{:S(2)}) %all-to-all-start.4) | async-done | bytes 8388640 | tf_op jit(solution)/shard_map/all_to_all | solution.py:354
  709.1 27.1 %back.1 = f32[32,32,64,128]{3,2,1,0:T(8,128)} custom-call(bf16[8,32,16,1024]{3,2,1,0:T(8,128)(2,1)} %bitcast.47.in_ref, bf16[256,128]{1,0:T(8,128)(2,1)S(1)} %bitcast.143), custom_call_target="tpu_custom_call" | custom-call | tf_op jit(solution)/shard_map/back/pallas_call | solution.py:356
  736.2 17.1 %gather_fusion.1 = f32[256,64,128]{2,1,0:T(8,128)} fusion(f32[1024,64,128]{2,1,0:T(8,128)} %bitcast.145, s32[1024]{0:T(1024)S(1)} %pad_clamp_fusion.1), kind=kCustom, calls=%fused_computation.1 | custom fusion | bytes 16778240 | tf_op jit(solution)/shard_map/gather | solution.py:372
  753.3 37.2 %points.1 = bf16[256,16,128]{2,1,0:T(8,128)(2,1)S(1)} custom-call(bf16[256,32,128]{2,1,0:T(8,128)(2,1)S(1)} %all-to-all-done.recv_ref, f32[256,64,128]{2,1,0:T(8,128)} %gather_fusion.1, bf16[256,64,128]{2,1,0:T(8,128)(2,1)} %bitcast.154, bf16[128,128]{1,0:T(8,128)(2,1)S(1)} %mul.535.skip_ref, bf16[128,512]{1,0:T(8,128)(2,1)S(1)} %mul.539.in_ref, ...), custom_call_target="tpu_custom_call" | custom-call | tf_op jit(solution)/shard_map/points/pallas_call | solution.py:374
  796.0 27.6 %all-to-all-done.5 = bf16[256,16,128]{2,1,0:T(8,128)(2,1)S(1)} async-done(((bf16[256,16,128]{2,1,0:T(8,128)(2,1)}), bf16[256,16,128]{2,1,0:T(8,128)(2,1)S(1)}, u32[]{:S(2)}, u32[]{:S(2)}) %all-to-all-start.5) | async-done | bytes 1048608 | tf_op jit(solution)/shard_map/all_to_all | solution.py:399
  (94 shorter events, 59.6 us)
Async XLA Ops:
  0.0 5.0 copy-start
  0.0 7.5 copy-start.4
  13.9 57.6 %all-to-all-start = ((bf16[256,32,128]{2,1,0:T(8,128)(2,1)}), bf16[256,32,128]{2,1,0:T(8,128)(2,1)S(1)}, u32[]{:S(2)}, u32[]{:S(2)}) async-start(bf16[256,32,128]{2,1,0:T(8,128)(2,1)} %broadcast_select_fusion), calls=%async_computation | async-start | bytes 4194304 | tf_op jit(solution)/shard_map/all_to_all | solution.py:257
  118.0 2.0 copy-start.3
  120.0 188.6 %all-to-all-start.1 = ((bf16[8,4,8,16,1024]{4,3,2,1,0:T(8,128)(2,1)}), bf16[8,4,8,16,1024]{4,3,2,1,0:T(8,128)(2,1)}, u32[]{:S(2)}, u32[]{:S(2)}) async-start(bf16[8,4,8,16,1024]{4,3,2,1,0:T(8,128)(2,1)} %get-tuple-element.7), calls=%async_computation.1 | async-start | bytes 16777216 | tf_op jit(solution)/shard_map/all_to_all | solution.py:306
  345.7 30.4 %all-to-all-start.2 = ((bf16[4,2,131072]{2,1,0:T(2,128)(2,1)}), bf16[4,2,131072]{2,1,0:T(2,128)(2,1)}, u32[]{:S(2)}, u32[]{:S(2)}) async-start(bf16[4,2,131072]{2,1,0:T(2,128)(2,1)} %reshape.994), calls=%async_computation.2 | async-start | bytes 4194304 | tf_op jit(solution)/shard_map/all_to_all | solution.py:321
  444.5 30.5 %all-to-all-start.3 = ((bf16[4,2,131072]{2,1,0:T(2,128)(2,1)}), bf16[4,2,131072]{2,1,0:T(2,128)(2,1)}, u32[]{:S(2)}, u32[]{:S(2)}) async-start(bf16[4,2,131072]{2,1,0:T(2,128)(2,1)} %reshape.996), calls=%async_computation.3 | async-start | bytes 4194304 | tf_op jit(solution)/shard_map/all_to_all | solution.py:344
  520.6 5.9 copy-start.6
  520.6 188.5 %all-to-all-start.4 = ((bf16[256,16,1024]{2,1,0:T(8,128)(2,1)}), bf16[256,16,1024]{2,1,0:T(8,128)(2,1)}, u32[]{:S(2)}, u32[]{:S(2)}) async-start(bf16[256,16,1024]{2,1,0:T(8,128)(2,1)} %bitcast.148), calls=%async_computation.4 | async-start | bytes 16777216 | tf_op jit(solution)/shard_map/all_to_all | solution.py:354
  526.6 5.1 copy-start.5
  531.8 5.8 copy-start.7
  533.4 4.9 copy-start.8
  753.3 71.8 %copy-start.1 = (bf16[16,16384]{1,0:T(8,128)(2,1)S(1)}, bf16[16,16384]{1,0:T(8,128)(2,1)}, u32[]{:S(2)}) copy-start(bf16[16,16384]{1,0:T(8,128)(2,1)} %param.10) | copy-start | bytes 1572868
  790.4 1.0 copy-start.2
  791.4 4.6 copy-start.9
  791.4 32.2 %all-to-all-start.5 = ((bf16[256,16,128]{2,1,0:T(8,128)(2,1)}), bf16[256,16,128]{2,1,0:T(8,128)(2,1)S(1)}, u32[]{:S(2)}, u32[]{:S(2)}) async-start(bf16[256,16,128]{2,1,0:T(8,128)(2,1)} %copy-done.2), calls=%async_computation.5 | async-start | bytes 2097152 | tf_op jit(solution)/shard_map/all_to_all | solution.py:399
